TPU v7x, 32 devices: a whole 2x2x4 slice. The times are simulated.
32 devices in a mesh: chan: 8 (over z, core), freq: 4 (over y, x).
Axes of the slice: x: 2, y: 2, z: 4, core: 2. Of those that a mesh axis runs over, the one named last changes fastest.
Arguments:
- records: bfloat16 [33792, 4096], P('freq', 'chan')
- offsets: int32 [256], P('freq'), may hold values from 0 to 8192, as said below
- dead_mask: int32 [4096], P('chan'), may hold values 0 or 1
- band_blocks: int32 [8], P('chan'), may hold values from 0 to 2, as said below
Outputs:
- cross: bfloat16 [3, 32, 4096, 1024], P(None, 'freq', 'chan')
Inputs may be any that keep to these rules, and one draw needn't show every extreme that they name: offsets[s] is the first sample of segment s within time block s // 64 of 8448 samples; all 256 samples of the segment lie in that block. band_blocks[b] is the largest block offset whose cross-spectra are kept for channel block b.
All inputs are finite; a program needn't handle non-finite values. No bound on the sum of `dead_mask` on one device may be relied on, other than what follows from the above.
Results may differ from a plain program's by a relative error of at most 0.0055.
Values may be sent and summed in bfloat16 or wider, within the bound.
A program may use at most 128 MiB of HBM per device.

v0:
```python
import jax
import jax.numpy as jnp
from jax import lax
from jax.sharding import PartitionSpec as P

SEG_LEN = 256
BINS = 32
FIRST_BIN = 2


EPS_POWER = 1e-06


def from_behind(block, axis, distance):
    devices = range(lax.axis_size(axis))
    route = [(i - distance, i) for i in devices if i - distance in devices]
    return lax.ppermute(block, axis, route)


def dft_table(seg_length, bin_count, first_bin):
    sample_index = jnp.arange(seg_length, dtype=jnp.int32)
    row_index = jnp.arange(2 * bin_count, dtype=jnp.int32)
    harmonic = row_index // 2 + first_bin
    phase_steps = harmonic[:, None] * sample_index[None, :] % seg_length
    phase_angle = 2.0 * jnp.pi / seg_length * phase_steps.astype(jnp.float32)
    hann_taper = 0.5 - 0.5 * jnp.cos(2.0 * jnp.pi / seg_length * sample_index.astype(jnp.float32))
    wave_rows = jnp.where(
        (row_index % 2 == 0)[:, None], jnp.cos(phase_angle), -jnp.sin(phase_angle)
    )
    return (hann_taper[None, :] * wave_rows).astype(jnp.bfloat16)


def local_products(left_panel, partner_panels):
    seg_count = left_panel.shape[2]
    left_real = left_panel[:, 0]
    left_imag = left_panel[:, 1]
    results = []
    for right_panel in partner_panels:
        real_part = jnp.einsum(
            "fpsi,fpsj->fij", left_panel, right_panel, preferred_element_type=jnp.float32
        )
        imag_part = jnp.einsum(
            "fsi,fsj->fij", left_imag, right_panel[:, 0], preferred_element_type=jnp.float32
        ) - jnp.einsum(
            "fsi,fsj->fij", left_real, right_panel[:, 1], preferred_element_type=jnp.float32
        )
        results.append(jnp.concatenate([real_part, imag_part], axis=2) * (1.0 / seg_count))
    return results


def shards(records, offsets, dead_mask, band_blocks):
    dft_rows = dft_table(SEG_LEN, BINS, FIRST_BIN)
    sample_rows = offsets[:, None] + jnp.arange(SEG_LEN, dtype=jnp.int32)[None, :]
    frames = jnp.take(records, sample_rows, axis=0)
    spectra = jnp.einsum("kt,stc->ksc", dft_rows, frames, preferred_element_type=jnp.float32)
    band_power = jnp.sum(spectra * spectra, axis=0) * (1.0 / BINS)
    scaling = dead_mask.astype(jnp.float32)[None, :] / jnp.sqrt(band_power + EPS_POWER)
    whitened = (spectra * scaling[None]).astype(jnp.bfloat16)
    whitened = whitened.reshape(BINS, 2, whitened.shape[1], whitened.shape[2])
    own_panel = lax.all_to_all(whitened, "freq", split_axis=0, concat_axis=2, tiled=True)
    upper_panel = from_behind(own_panel, "chan", -1)
    second_panel = from_behind(own_panel, "chan", -2)
    products = local_products(own_panel, [own_panel, upper_panel, second_panel])
    band_limit = band_blocks[0]
    results = []
    for offset_index, product in enumerate(products):
        keep_flag = (offset_index <= band_limit).astype(jnp.bfloat16)
        results.append(product.astype(jnp.bfloat16) * keep_flag)
    return jnp.stack(results, axis=0)


def solution(mesh):
    in_specs = (P("freq", "chan"), P("freq"), P("chan"), P("chan"))
    out_specs = P(None, "freq", "chan", None)
    return jax.shard_map(shards, mesh=mesh, in_specs=in_specs, out_specs=out_specs, check_vma=False)
```

profile of v0, /device:TPU:0, one launch (start us, length us, event | category | flops | bytes accessed | tf_op | source)
XLA Modules:
  0.0 363.4 jit_solution(15902509209407898072)
XLA Ops:
  0.1 0.7 fusion.22
  0.8 0.7 fusion.16
  1.6 0.7 convert_element_type.70
  2.3 71.3 %gather_fusion = bf16[16384,512]{1,0:T(8,128)(2,1)} fusion(bf16[8448,512]{1,0:T(8,128)(2,1)} %param.4, s32[16384]{0:T(1024)S(1)} %broadcast_clamp_fusion), kind=kCustom, calls=%fused_computation | custom fusion | bytes 33619968 | tf_op jit(solution)/shard_map/jit(_take)/gather | solution.py:54
  73.6 9.3 %multiply_reduce_fusion = (f32[64,512]{1,0:T(8,128)S(1)}, f32[64,64,512]{2,0,1:T(8,128)S(1)}) fusion(bf16[64,256,512]{2,1,0:T(8,128)(2,1)} %bitcast.82, pred[64,256]{1,0:T(8,128)(4,1)S(1)} %fusion.22, s32[64]{0:T(128)S(1)} %fusion.33, f32[256]{0:T(256)S(1)} %multiply_subtract_fusion, pred[64]{0:T(512)(128)(4,1)S(1)} %fusion.32), kind=kOutput, calls=%fused_computation.18 | convolution fusion | flops 1086586880 | bytes 25314624 | tf_op jit(solution)/shard_map/kt,stc->ksc/dot_general | solution.py:55
  83.0 1.6 multiply_convert_fusion
  84.5 2.4 copy.46
  86.9 52.8 %all_to_all.18 = bf16[32,2,64,512]{3,2,1,0:T(8,128)(2,1)S(1)} all-to-all(bf16[32,2,64,512]{3,2,1,0:T(8,128)(2,1)S(1)} %bitcast.83), channel_id=1, replica_groups=mesh['chan'=8,'freq'=4] {'freq'}, dimensions={0} | all-to-all | bytes 8388608 | tf_op jit(solution)/shard_map/all_to_all | solution.py:60
  139.7 2.5 copy.27
  142.2 6.5 %copy.33 = bf16[8,2,256,512]{2,3,1,0:T(8,128)(2,1)} copy(bf16[8,2,256,512]{3,2,1,0:T(8,128)(2,1)} %bitcast.72) | data formatting | bytes 8388608 | tf_op jit(solution)/shard_map/all_to_all | solution.py:60
  148.7 1.3 collective-permute-start
  150.7 0.0 copy-start
  150.7 1.7 collective-permute-start.1
  152.4 5.8 %convolution_bitcast_fusion.2 = f32[1,8,512,512]{2,3,1,0:T(8,128)S(1)} fusion(bf16[8,2,256,512]{3,2,1,0:T(8,128)(2,1)} %bitcast.73), kind=kOutput, calls=%fused_computation.22 | convolution fusion | flops 2147483648 | bytes 12582912 | tf_op jit(solution)/shard_map/fpsi,fpsj->fij/dot_general | solution.py:39
  158.3 0.0 copy-done
  158.3 4.7 %fusion.12 = f32[8,512,512]{1,2,0:T(8,128)} fusion(bf16[8,2,256,512]{3,2,1,0:T(8,128)(2,1)S(1)} %bitcast.74), kind=kOutput, calls=%fused_computation.31 | convolution fusion | flops 1073741824 | bytes 12582912 | tf_op jit(solution)/shard_map/fsi,fsj->fij/dot_general | solution.py:44
  163.0 8.1 %subtract_bitcast_fusion.2 = f32[1,8,512,512]{2,3,1,0:T(8,128)} fusion(f32[8,512,512]{1,2,0:T(8,128)} %fusion.12, bf16[8,2,256,512]{3,2,1,0:T(8,128)(2,1)S(1)} %bitcast.75), kind=kOutput, calls=%fused_computation.16 | convolution fusion | flops 1075838976 | bytes 20971520 | tf_op jit(solution)/shard_map/fsi,fsj->fij/dot_general | solution.py:42
  171.1 7.9 %fusion.8 = bf16[1,8,512,1024]{2,3,1,0:T(8,128)(2,1)} fusion(f32[1,8,512,512]{2,3,1,0:T(8,128)} %subtract_bitcast_fusion.2, f32[1,8,512,512]{2,3,1,0:T(8,128)S(1)} %convolution_bitcast_fusion.2, bf16[]{:T(256)} %bitcast.12), kind=kLoop, calls=%fused_computation.13 | loop fusion | flops 16777216 | bytes 25165826 | tf_op jit(solution)/shard_map/mul | solution.py:68
  178.9 0.0 collective-permute-done
  179.0 4.7 %fusion.11 = f32[8,512,512]{1,2,0:T(8,128)} fusion(bf16[8,2,256,512]{2,3,1,0:T(8,128)(2,1)S(1)} %collective-permute-done, bf16[8,2,256,512]{3,2,1,0:T(8,128)(2,1)S(1)} %bitcast.76), kind=kOutput, calls=%fused_computation.27 | convolution fusion | flops 1073741824 | bytes 12582912 | tf_op jit(solution)/shard_map/fsi,fsj->fij/dot_general | solution.py:44
  183.6 2.3 convolution_bitcast_fusion.1
  185.9 4.7 %subtract_bitcast_fusion.1 = f32[1,8,512,512]{2,3,1,0:T(8,128)S(1)} fusion(f32[8,512,512]{1,2,0:T(8,128)} %fusion.11, bf16[8,2,256,512]{2,3,1,0:T(8,128)(2,1)S(1)} %collective-permute-done, bf16[8,2,256,512]{3,2,1,0:T(8,128)(2,1)S(1)} %bitcast.78), kind=kOutput, calls=%fused_computation.15 | convolution fusion | flops 1075838976 | bytes 20971520 | tf_op jit(solution)/shard_map/fsi,fsj->fij/dot_general | solution.py:42
  190.7 4.7 %fusion.7 = bf16[1,8,512,1024]{2,3,1,0:T(8,128)(2,1)} fusion(f32[1,8,512,512]{2,3,1,0:T(8,128)S(1)} %subtract_bitcast_fusion.1, f32[1,8,512,512]{2,3,1,0:T(8,128)S(1)} %convolution_bitcast_fusion.1, bf16[]{:T(256)} %bitcast.19), kind=kLoop, calls=%fused_computation.12 | loop fusion | flops 16777216 | bytes 25165826 | tf_op jit(solution)/shard_map/mul | solution.py:68
  195.3 93.5 %collective-permute-done.1 = bf16[8,2,256,512]{2,3,1,0:T(8,128)(2,1)} collective-permute-done((bf16[8,2,256,512]{2,3,1,0:T(8,128)(2,1)}, bf16[8,2,256,512]{2,3,1,0:T(8,128)(2,1)}, u32[]{:S(2)}, u32[]{:S(2)}) %collective-permute-start.1) | collective-permute-done | bytes 4194336 | tf_op jit(solution)/shard_map/ppermute | solution.py:17
  288.9 6.2 %fusion.10 = f32[8,512,512]{1,2,0:T(8,128)} fusion(bf16[8,2,256,512]{2,3,1,0:T(8,128)(2,1)} %collective-permute-done.1, bf16[8,2,256,512]{3,2,1,0:T(8,128)(2,1)S(1)} %bitcast.79), kind=kOutput, calls=%fused_computation.24 | convolution fusion | flops 1073741824 | bytes 12582912 | tf_op jit(solution)/shard_map/fsi,fsj->fij/dot_general | solution.py:44
  295.1 4.5 %convolution_bitcast_fusion = f32[1,8,512,512]{2,3,1,0:T(8,128)S(1)} fusion(bf16[8,2,256,512]{2,3,1,0:T(8,128)(2,1)} %collective-permute-done.1, bf16[8,2,256,512]{3,2,1,0:T(8,128)(2,1)S(1)} %bitcast.80), kind=kOutput, calls=%fused_computation.20 | convolution fusion | flops 2147483648 | bytes 16777216 | tf_op jit(solution)/shard_map/fpsi,fpsj->fij/dot_general | solution.py:39
  299.6 5.3 %subtract_bitcast_fusion = f32[1,8,512,512]{2,3,1,0:T(8,128)S(1)} fusion(f32[8,512,512]{1,2,0:T(8,128)} %fusion.10, bf16[8,2,256,512]{2,3,1,0:T(8,128)(2,1)} %collective-permute-done.1, bf16[8,2,256,512]{3,2,1,0:T(8,128)(2,1)S(1)} %bitcast.81), kind=kOutput, calls=%fused_computation.14 | convolution fusion | flops 1075838976 | bytes 20971520 | tf_op jit(solution)/shard_map/fsi,fsj->fij/dot_general | solution.py:42
  304.9 4.6 %fusion.6 = bf16[1,8,512,1024]{2,3,1,0:T(8,128)(2,1)} fusion(f32[1,8,512,512]{2,3,1,0:T(8,128)S(1)} %subtract_bitcast_fusion, f32[1,8,512,512]{2,3,1,0:T(8,128)S(1)} %convolution_bitcast_fusion, bf16[]{:T(256)} %bitcast.26), kind=kLoop, calls=%fused_computation.11 | loop fusion | flops 16777216 | bytes 25165826 | tf_op jit(solution)/shard_map/mul | solution.py:68
  309.6 20.7 %pad_maximum_fusion = bf16[3,8,512,1024]{2,3,1,0:T(8,128)(2,1)} fusion(bf16[1,8,512,1024]{2,3,1,0:T(8,128)(2,1)} %fusion.6, bf16[1,8,512,1024]{2,3,1,0:T(8,128)(2,1)} %fusion.7, bf16[1,8,512,1024]{2,3,1,0:T(8,128)(2,1)} %fusion.8), kind=kLoop, calls=%fused_computation.1 | loop fusion | flops 25165824 | bytes 50331648 | tf_op jit(solution)/shard_map/stack | solution.py:69
  330.2 33.2 %copy.37 = bf16[3,8,512,1024]{3,2,1,0:T(8,128)(2,1)} copy(bf16[3,8,512,1024]{2,3,1,0:T(8,128)(2,1)} %pad_maximum_fusion) | data formatting | bytes 50331648 | tf_op jit(solution)/shard_map/stack | solution.py:69
  (6 shorter events, 0.1 us)
Async XLA Ops:
  148.7 30.2 %collective-permute-start = (bf16[8,2,256,512]{2,3,1,0:T(8,128)(2,1)}, bf16[8,2,256,512]{2,3,1,0:T(8,128)(2,1)S(1)}, u32[]{:S(2)}, u32[]{:S(2)}) collective-permute-start(bf16[8,2,256,512]{2,3,1,0:T(8,128)(2,1)} %copy.33), channel_id=1, source_target_pairs={{4,0},{8,4},{12,8},{16,12},{20,16},{24,20},{28,24},{5,1},{9,5},{13... | collective-permute-start | bytes 12582920 | tf_op jit(solution)/shard_map/ppermute | solution.py:17
  150.7 7.6 %copy-start = (bf16[8,2,4,64,512]{4,3,2,1,0:T(8,128)(2,1)S(1)}, bf16[8,2,4,64,512]{4,3,2,1,0:T(8,128)(2,1)}, u32[]{:S(2)}) copy-start(bf16[8,2,4,64,512]{4,3,2,1,0:T(8,128)(2,1)} %copy.27) | copy-start | bytes 12582916
  150.7 138.2 %collective-permute-start.1 = (bf16[8,2,256,512]{2,3,1,0:T(8,128)(2,1)}, bf16[8,2,256,512]{2,3,1,0:T(8,128)(2,1)}, u32[]{:S(2)}, u32[]{:S(2)}) collective-permute-start(bf16[8,2,256,512]{2,3,1,0:T(8,128)(2,1)} %copy.33), channel_id=1, source_target_pairs={{8,0},{12,4},{16,8},{20,12},{24,16},{28,20},{9,1},{13,5},{17,9},{2... | collective-permute-start | bytes 12582920 | tf_op jit(solution)/shard_map/ppermute | solution.py:17
where the time goes:
time: 365 us; the launch traced here: 363 us
  local copies, waits for them, and re-layouts  116 us (32%)
  waiting for transfers between devices  93.5 us (26%)
  matrix products  55.6 us (15%)
  blocking collectives  52.8 us (14%)
  other arithmetic  41.7 us (11%)
    ppermute x2, waiting for transfers between devices, from_behind(): return lax.ppermute(block, axis, route)  93.5 us
    gather x1, local copies, waits for them, and re-layouts, shards(): frames = jnp.take(records, sample_rows, axis=0)  71.3 us
    all_to_all x1, blocking collectives, shards(): lax.all_to_all(whitened, 'freq', split_axis=0, concat_axis=2, tiled=True)  52.8 us
    another operation x1, local copies, waits for them, and re-layouts, shards(): return jnp.stack(results, axis=0)  33.2 us
    another operation x1, other arithmetic, shards(): return jnp.stack(results, axis=0)  20.7 us
    dot_general x3, matrix products, local_products(): jnp.einsum('fsi,fsj->fij', left_imag, right_panel[:, 0], preferred_elemen...  18.1 us
    mul x3, other arithmetic, shards(): results.append(product.astype(jnp.bfloat16) * keep_flag)  17.2 us
    dot_general x3, matrix products, local_products(): jnp.einsum('fsi,fsj->fij', left_real, right_panel[:, 1], preferred_elemen...  15.6 us
  transfers between devices with their start and end apart: 2, of which 1 were waited for; matrix products, arithmetic and copies ran while one was open for 12% of the time, Pallas kernels for 0%

commit v1 on v0

v1 whole, which is shorter than its diff:
```python
import functools

import jax
import jax.numpy as jnp
import ml_dtypes
import numpy as np
from jax import lax
from jax.experimental import pallas as pl
from jax.experimental.pallas import tpu as pltpu
from jax.sharding import PartitionSpec as P

SEG_LEN = 256
BINS = 32
FIRST_BIN = 2
ROWS = 2 * BINS
ALIGN = 16
LANES = 128
BAND = 2

EPS_POWER = 1e-06
MESH = pl.DeviceIdType.MESH
MIB = 1024 * 1024


def dft_tables(seg_length, bin_count, first_bin, shifts):
    sample_index = np.arange(seg_length)
    row_index = np.arange(2 * bin_count)
    harmonic = row_index // 2 + first_bin
    phase_steps = harmonic[:, None] * sample_index[None, :] % seg_length
    phase_angle = np.float32(2.0 * np.pi / seg_length) * phase_steps.astype(np.float32)
    taper_angle = np.float32(2.0 * np.pi / seg_length) * sample_index.astype(np.float32)
    hann_taper = np.float32(0.5) - np.float32(0.5) * np.cos(taper_angle)
    wave_rows = np.where((row_index % 2 == 0)[:, None], np.cos(phase_angle), -np.sin(phase_angle))
    table = (hann_taper[None, :] * wave_rows).astype(ml_dtypes.bfloat16)
    return np.stack([np.roll(table, m, axis=1) for m in range(shifts)], axis=0)


def whiten_kernel(offs_ref, x_ref, tab_ref, mask_ref, w_ref, flat_ref):
    seg_count = offs_ref.shape[0]
    cols = x_ref.shape[1]
    row = lax.broadcasted_iota(jnp.int32, (ALIGN, cols), 0)
    live = mask_ref[...].astype(jnp.float32)

    def segment(s, carry):
        start = offs_ref[s]
        m = lax.rem(start, ALIGN)
        base = pl.multiple_of(start - m, ALIGN)
        after = pl.multiple_of(jnp.minimum(base + SEG_LEN, x_ref.shape[0] - ALIGN), ALIGN)
        head = jnp.where(row >= m, x_ref[pl.ds(base, ALIGN), :], x_ref[pl.ds(after, ALIGN), :])
        body = x_ref[pl.ds(pl.multiple_of(base + ALIGN, ALIGN), SEG_LEN - ALIGN), :]
        frame = jnp.concatenate([head, body], axis=0)
        spectra = jnp.dot(tab_ref[m], frame, preferred_element_type=jnp.float32)
        power = jnp.sum(spectra * spectra, axis=0, keepdims=True) * (1.0 / BINS)
        scaled = spectra * (live / jnp.sqrt(power + EPS_POWER))
        for j in range(cols // LANES):
            flat_ref[j, pl.ds(s, ROWS, stride=seg_count), :] = scaled[:, j * LANES:(j + 1) * LANES]
        return carry

    lax.fori_loop(0, seg_count, segment, 0, unroll=2)

    def pack(r, carry):
        at = pl.ds(pl.multiple_of(r * seg_count, seg_count), seg_count)
        for j in range(cols // LANES):
            w_ref[r, :, j * LANES:(j + 1) * LANES] = flat_ref[j, at, :].astype(jnp.bfloat16)
        return carry

    lax.fori_loop(0, ROWS, pack, 0)


def whiten(records, offsets, dead_mask):
    seg_count = offsets.shape[0]
    cols = records.shape[1]
    tables = jnp.asarray(dft_tables(SEG_LEN, BINS, FIRST_BIN, ALIGN))
    vmem = pl.BlockSpec(memory_space=pltpu.VMEM)
    return pl.pallas_call(
        whiten_kernel,
        out_shape=jax.ShapeDtypeStruct((ROWS, seg_count, cols), jnp.bfloat16),
        in_specs=[pl.BlockSpec(memory_space=pltpu.SMEM), vmem, vmem, vmem],
        out_specs=vmem,
        scratch_shapes=[pltpu.VMEM((cols // LANES, ROWS * seg_count, LANES), jnp.float32)],
        compiler_params=pltpu.CompilerParams(vmem_limit_bytes=40 * MIB),
        cost_estimate=pl.CostEstimate(
            flops=2 * ROWS * SEG_LEN * cols * seg_count, bytes_accessed=13 * MIB, transcendentals=0
        ),
        name="whiten",
    )(offsets, records, tables, dead_mask.reshape(1, cols))


def peer_of(f, k):
    flipped = f
    bit = 1
    while bit <= k:
        if k & bit:
            flipped = flipped + bit - 2 * bit * ((f // bit) % 2)
        bit *= 2
    return flipped


def exchange_kernel(nchan, nfreq, chunks, w_ref, own_ref, up_ref, far_ref,
                    a_send, a_recv, z_send, z_recv, c_send, c_recv, l_sem):
    b = lax.axis_index("chan")
    f = lax.axis_index("freq")
    core = b % 2
    has_low = b >= 2
    has_high = b + 2 < nchan
    other = b + 1 - 2 * core
    per = own_ref.shape[1] // chunks

    barrier = pltpu.get_barrier_semaphore()
    for k in range(1, nfreq):
        pl.semaphore_signal(barrier, inc=1, device_id=(b, peer_of(f, k)), device_id_type=MESH)
    pl.semaphore_signal(barrier, inc=1, device_id=(other, f), device_id_type=MESH)

    @pl.when(has_low)
    def _():
        pl.semaphore_signal(barrier, inc=1, device_id=(b - 2, f), device_id_type=MESH)

    @pl.when(has_high)
    def _():
        pl.semaphore_signal(barrier, inc=1, device_id=(b + 2, f), device_id_type=MESH)

    greeted = nfreq + has_low.astype(jnp.int32) + has_high.astype(jnp.int32)
    pl.semaphore_wait(barrier, greeted)

    def rows(c):
        return pl.ds(c * per, per)

    def across(k, c):
        return pltpu.make_async_remote_copy(
            src_ref=w_ref.at[peer_of(f, k), rows(c)], dst_ref=own_ref.at[k, rows(c)],
            send_sem=a_send.at[k, c], recv_sem=a_recv.at[k, c],
            device_id=(b, peer_of(f, k)), device_id_type=MESH)

    def down(k, c):
        src = w_ref.at[f, rows(c)] if k == 0 else own_ref.at[k, rows(c)]
        return pltpu.make_async_remote_copy(
            src_ref=src, dst_ref=far_ref.at[k, rows(c)],
            send_sem=z_send.at[k, c], recv_sem=z_recv.at[k, c],
            device_id=(b - 2, f), device_id_type=MESH)

    def beside(src_ref, k, c):
        src = w_ref.at[f, rows(c)] if src_ref is None else src_ref.at[k, rows(c)]
        return pltpu.make_async_remote_copy(
            src_ref=src, dst_ref=up_ref.at[k, rows(c)],
            send_sem=c_send.at[k, c], recv_sem=c_recv.at[k, c],
            device_id=(other, f), device_id_type=MESH)

    for c in range(chunks):
        for k in range(1, nfreq):
            across(k, c).start()
    local = pltpu.make_async_copy(w_ref.at[f], own_ref.at[0], l_sem)
    local.start()

    for c in range(chunks):
        for k in range(nfreq):
            if k > 0:
                across(k, c).wait_recv()

            @pl.when(has_low)
            def _():
                down(k, c).start()

            @pl.when(core == 1)
            def _():
                beside(None if k == 0 else own_ref, k, c).start()

    for c in range(chunks):
        for k in range(nfreq):
            @pl.when(has_high)
            def _():
                down(k, c).wait_recv()

            @pl.when(has_high & (core == 0))
            def _():
                beside(far_ref, k, c).start()

    for c in range(chunks):
        for k in range(nfreq):
            if k > 0:
                across(k, c).wait_send()

            @pl.when(has_low)
            def _():
                down(k, c).wait_send()

            @pl.when(has_high | (core == 1))
            def _():
                beside(far_ref, k, c).wait_send()

            @pl.when(has_high | (core == 0))
            def _():
                beside(far_ref, k, c).wait_recv()

    local.wait()


def exchange(whitened, nchan, nfreq, chunks):
    _, seg_count, cols = whitened.shape
    mine = BINS // nfreq
    w = whitened.reshape(nfreq, mine, 2, seg_count, cols)
    panel = jax.ShapeDtypeStruct((nfreq, mine, 2, seg_count, cols), jnp.bfloat16)
    vmem = pl.BlockSpec(memory_space=pltpu.VMEM)
    pair = pltpu.SemaphoreType.DMA((nfreq, chunks))
    return pl.pallas_call(
        functools.partial(exchange_kernel, nchan, nfreq, chunks),
        out_shape=[panel] * 3,
        in_specs=[vmem],
        out_specs=[vmem] * 3,
        scratch_shapes=[pair] * 6 + [pltpu.SemaphoreType.DMA],
        compiler_params=pltpu.CompilerParams(
            collective_id=0, has_side_effects=True, vmem_limit_bytes=40 * MIB
        ),
        name="exchange",
    )(w)


def cross_kernel(keep_ref, own_ref, up_ref, far_ref, out_ref):
    nfreq, _, _, seg_count, cols = own_ref.shape
    depth = nfreq * 2 * seg_count
    scale = 1.0 / (nfreq * seg_count)
    left = own_ref[:, 0].reshape(depth, cols)
    turned = jnp.stack([own_ref[:, 0, 1], -own_ref[:, 0, 0]], axis=1).reshape(depth, cols)
    both = jnp.concatenate([left.T, turned.T], axis=0)
    for d, ref in enumerate((own_ref, up_ref, far_ref)):
        @pl.when(keep_ref[d] != 0)
        def _():
            right = ref[:, 0].reshape(depth, cols)
            product = jnp.dot(both, right, preferred_element_type=jnp.float32) * scale
            out_ref[d, 0, :, :cols] = product[:cols].astype(jnp.bfloat16)
            out_ref[d, 0, :, cols:] = product[cols:].astype(jnp.bfloat16)

        @pl.when(keep_ref[d] == 0)
        def _():
            out_ref[d] = jnp.zeros(out_ref.shape[1:], jnp.bfloat16)


def cross(keep, own, up, far):
    nfreq, mine, _, seg_count, cols = own.shape
    panel = pl.BlockSpec((nfreq, 1, 2, seg_count, cols), lambda i: (0, i, 0, 0, 0))
    return pl.pallas_call(
        cross_kernel,
        grid=(mine,),
        out_shape=jax.ShapeDtypeStruct((BAND + 1, mine, cols, 2 * cols), jnp.bfloat16),
        in_specs=[pl.BlockSpec(memory_space=pltpu.SMEM), panel, panel, panel],
        out_specs=pl.BlockSpec((BAND + 1, 1, cols, 2 * cols), lambda i: (0, i, 0, 0)),
        compiler_params=pltpu.CompilerParams(vmem_limit_bytes=40 * MIB),
        cost_estimate=pl.CostEstimate(
            flops=12 * mine * cols * cols * 2 * nfreq * seg_count, bytes_accessed=40 * MIB, transcendentals=0
        ),
        name="cross",
    )(keep, own, up, far)


def shards(nchan, nfreq, records, offsets, dead_mask, band_blocks):
    whitened = whiten(records, offsets, dead_mask)
    own, up, far = exchange(whitened, nchan, nfreq, 4)
    b = lax.axis_index("chan")
    offset = jnp.arange(BAND + 1, dtype=jnp.int32)
    keep = ((offset <= band_blocks[0]) & (b + offset < nchan)).astype(jnp.int32)
    return cross(keep, own, up, far)


def solution(mesh):
    in_specs = (P("freq", "chan"), P("freq"), P("chan"), P("chan"))
    out_specs = P(None, "freq", "chan", None)
    body = functools.partial(shards, mesh.shape["chan"], mesh.shape["freq"])
    return jax.shard_map(body, mesh=mesh, in_specs=in_specs, out_specs=out_specs, check_vma=False)
```

time: 365 us -> 149 us (0.41)
  the two profiles are of different devices: /device:TPU:0 before, /device:TPU:13 now
where the time goes in v1:
time: 149 us
  Pallas kernels  140 us (94%)
  local copies, waits for them, and re-layouts  7.84 us (5%)
    pallas_call x1, Pallas kernels, exchange(): pl.pallas_call(functools.partial(exchange_kernel, nchan, nfreq, chunks),...  99.5 us
    pallas_call x1, Pallas kernels, cross(): pl.pallas_call(cross_kernel, grid=(mine,), out_shape=jax.ShapeDtypeStruct...  22.9 us
    pallas_call x1, Pallas kernels, whiten(): pl.pallas_call(whiten_kernel, out_shape=jax.ShapeDtypeStruct((ROWS, seg_c...  17.7 us
    unnamed x10, local copies, waits for them, and re-layouts  7.84 us

profile of v1, /device:TPU:13, one launch (start us, length us, event | category | flops | bytes accessed | tf_op | source)
XLA Modules:
  0.0 148.6 jit_solution(4726800943981946636)
XLA Ops:
  0.7 0.0 copy-start.1
  0.7 3.4 %copy-done.1 = bf16[8448,512]{1,0:T(8,128)(2,1)S(1)} copy-done((bf16[8448,512]{1,0:T(8,128)(2,1)S(1)}, bf16[8448,512]{1,0:T(8,128)(2,1)}, u32[]{:S(2)}) %copy-start.1) | copy-done | bytes 8650776
  4.1 0.0 copy-start.2
  4.1 1.0 copy-done.2
  5.2 0.0 copy-start.3
  5.2 0.7 copy-done.3
  5.8 0.0 copy-start.4
  5.9 0.7 copy-done.4
  6.5 17.7 %whiten.1 = bf16[64,64,512]{2,1,0:T(8,128)(2,1)S(1)} custom-call(s32[64]{0:T(128)S(1)} %copy-done.4, bf16[8448,512]{1,0:T(8,128)(2,1)S(1)} %copy-done.1, bf16[16,64,256]{2,1,0:T(8,128)(2,1)S(1)} %copy-done.2, s32[1,512]{1,0:T(1,128)S(1)} %bitcast.5), custom_call_target="tpu_custom_call" | custom-call | flops 1073741824 | bytes 13631488 | tf_op jit(solution)/shard_map/whiten/pallas_call | solution.py:75
  24.2 0.0 copy-start
  24.2 2.0 %copy-done = bf16[64,64,512]{2,1,0:T(8,128)(2,1)} copy-done((bf16[64,64,512]{2,1,0:T(8,128)(2,1)}, bf16[64,64,512]{2,1,0:T(8,128)(2,1)S(1)}, u32[]{:S(2)}) %copy-start) | copy-done | bytes 4194328
  26.2 99.5 %exchange.1 = (bf16[4,8,2,64,512]{4,3,2,1,0:T(8,128)(2,1)S(1)}, bf16[4,8,2,64,512]{4,3,2,1,0:T(8,128)(2,1)S(1)}, bf16[4,8,2,64,512]{4,3,2,1,0:T(8,128)(2,1)S(1)}) custom-call(bf16[4,8,2,64,512]{4,3,2,1,0:T(8,128)(2,1)} %bitcast.4), custom_call_target="tpu_custom_call" | custom-call | tf_op jit(solution)/shard_map/exchange/pallas_call | solution.py:204
  125.7 22.9 %cross.1 = bf16[3,8,512,1024]{3,2,1,0:T(8,128)(2,1)} custom-call(s32[3]{0:T(128)S(1)} %and_convert_fusion.keep_ref, bf16[4,8,2,64,512]{4,3,2,1,0:T(8,128)(2,1)S(1)} %get-tuple-element.8.own_ref, bf16[4,8,2,64,512]{4,3,2,1,0:T(8,128)(2,1)S(1)} %get-tuple-element.9.up_ref, bf16[4,8,2,64,512]{4,3,2,1,0:T(8,128)(2,1)S(1)} %get-tuple-element.10.far_ref), custom_call_target="tpu_custom_call" | custom-call | flops 12884901888 | bytes 41943040 | tf_op jit(solution)/shard_map/cross/pallas_call | solution.py:240
  (1 shorter events, 0.0 us)
Async XLA Ops:
  0.7 3.5 %copy-start.1 = (bf16[8448,512]{1,0:T(8,128)(2,1)S(1)}, bf16[8448,512]{1,0:T(8,128)(2,1)}, u32[]{:S(2)}) copy-start(bf16[8448,512]{1,0:T(8,128)(2,1)} %x_ref.1) | copy-start | bytes 25952260
  4.1 1.0 copy-start.2
  5.2 0.7 copy-start.3
  5.8 0.7 copy-start.4
  24.2 2.0 %copy-start = (bf16[64,64,512]{2,1,0:T(8,128)(2,1)}, bf16[64,64,512]{2,1,0:T(8,128)(2,1)S(1)}, u32[]{:S(2)}) copy-start(bf16[64,64,512]{2,1,0:T(8,128)(2,1)S(1)} %whiten.1) | copy-start | bytes 12582916

commit v2 on v1

v2 whole, which is shorter than its diff:
```python
import functools

import jax
import jax.numpy as jnp
import ml_dtypes
import numpy as np
from jax import lax
from jax.experimental import pallas as pl
from jax.experimental.pallas import tpu as pltpu
from jax.sharding import PartitionSpec as P

SEG_LEN = 256
BINS = 32
FIRST_BIN = 2
ROWS = 2 * BINS
ALIGN = 16
LANES = 128
GROUP = 16
CHUNKS = 4
BAND = 2

EPS_POWER = 1e-06
MESH = pl.DeviceIdType.MESH
MIB = 1024 * 1024


def dft_tables(seg_length, bin_count, first_bin, shifts):
    sample_index = np.arange(seg_length)
    row_index = np.arange(2 * bin_count)
    harmonic = row_index // 2 + first_bin
    phase_steps = harmonic[:, None] * sample_index[None, :] % seg_length
    phase_angle = np.float32(2.0 * np.pi / seg_length) * phase_steps.astype(np.float32)
    taper_angle = np.float32(2.0 * np.pi / seg_length) * sample_index.astype(np.float32)
    hann_taper = np.float32(0.5) - np.float32(0.5) * np.cos(taper_angle)
    wave_rows = np.where((row_index % 2 == 0)[:, None], np.cos(phase_angle), -np.sin(phase_angle))
    table = (hann_taper[None, :] * wave_rows).astype(ml_dtypes.bfloat16)
    return np.stack([np.roll(table, m, axis=1) for m in range(shifts)], axis=0)


def whiten_kernel(offs_ref, x_ref, tab_ref, mask_ref, w_ref, flat_ref):
    seg_count = offs_ref.shape[0]
    cols = x_ref.shape[1]
    row = lax.broadcasted_iota(jnp.int32, (ALIGN, cols), 0)
    live = mask_ref[...].astype(jnp.float32)

    def whiten_group(g, carry):
        def segment(s, carry):
            start = offs_ref[g * GROUP + s]
            m = start % ALIGN
            base = pl.multiple_of(start - m, ALIGN)
            after = pl.multiple_of(jnp.minimum(base + SEG_LEN, x_ref.shape[0] - ALIGN), ALIGN)
            head = jnp.where(row >= m, x_ref[pl.ds(base, ALIGN), :], x_ref[pl.ds(after, ALIGN), :])
            body = x_ref[pl.ds(pl.multiple_of(base + ALIGN, ALIGN), SEG_LEN - ALIGN), :]
            frame = jnp.concatenate([head, body], axis=0)
            spectra = jnp.dot(tab_ref[m], frame, preferred_element_type=jnp.float32)
            power = jnp.sum(spectra * spectra, axis=0, keepdims=True) * (1.0 / BINS)
            scaled = spectra * (live * lax.rsqrt(power + EPS_POWER))
            for j in range(cols // LANES):
                flat_ref[j, pl.ds(s, ROWS, stride=GROUP), :] = scaled[:, j * LANES:(j + 1) * LANES]
            return carry

        lax.fori_loop(0, GROUP, segment, 0, unroll=4)

        def pack(r, carry):
            at = pl.ds(pl.multiple_of(r * GROUP, GROUP), GROUP)
            for j in range(cols // LANES):
                w_ref[r, pl.ds(pl.multiple_of(g * GROUP, GROUP), GROUP), j * LANES:(j + 1) * LANES] = flat_ref[j, at, :].astype(jnp.bfloat16)
            return carry

        lax.fori_loop(0, ROWS, pack, 0, unroll=4)
        return carry

    lax.fori_loop(0, seg_count // GROUP, whiten_group, 0)


def whiten(records, offsets, dead_mask):
    seg_count = offsets.shape[0]
    cols = records.shape[1]
    tables = jnp.asarray(dft_tables(SEG_LEN, BINS, FIRST_BIN, ALIGN))
    vmem = pl.BlockSpec(memory_space=pltpu.VMEM)
    return pl.pallas_call(
        whiten_kernel,
        out_shape=jax.ShapeDtypeStruct((ROWS, seg_count, cols), jnp.bfloat16),
        in_specs=[pl.BlockSpec(memory_space=pltpu.SMEM), vmem, vmem, vmem],
        out_specs=vmem,
        scratch_shapes=[pltpu.VMEM((cols // LANES, ROWS * GROUP, LANES), jnp.float32)],
        compiler_params=pltpu.CompilerParams(vmem_limit_bytes=24 * MIB),
        cost_estimate=pl.CostEstimate(
            flops=2 * ROWS * SEG_LEN * cols * seg_count, bytes_accessed=13 * MIB, transcendentals=0
        ),
        name="whiten",
    )(offsets, records, tables, dead_mask.reshape(1, cols))


def peer_of(f, k):
    flipped = f
    bit = 1
    while bit <= k:
        if k & bit:
            flipped = flipped + bit - 2 * bit * ((f // bit) % 2)
        bit *= 2
    return flipped


def product(own_ref, right_ref, i, out_ref, *at):
    nfreq, _, seg_count, cols = own_ref.shape
    depth = nfreq * 2 * seg_count
    scale = 1.0 / (nfreq * seg_count)
    pair = own_ref[:, pl.ds(2 * i, 2)]
    left = pair.reshape(depth, cols)
    turned = jnp.stack([pair[:, 1], -pair[:, 0]], axis=1).reshape(depth, cols)
    both = jnp.concatenate([left.T, turned.T], axis=0)
    right = right_ref[:, pl.ds(2 * i, 2)].reshape(depth, cols)
    result = jnp.dot(both, right, preferred_element_type=jnp.float32) * scale
    out_ref[(*at, slice(None), slice(0, cols))] = result[:cols].astype(jnp.bfloat16)
    out_ref[(*at, slice(None), slice(cols, 2 * cols))] = result[cols:].astype(jnp.bfloat16)


def exchange_kernel(nchan, nfreq, chunks, w_ref,
                    own_ref, up_ref, far_ref, first_ref, second_ref, third_ref,
                    a_send, a_recv, z_send, z_recv, c_send, c_recv,
                    z0_send, z0_recv, c0_send, c0_recv, l_sem):
    b = lax.axis_index("chan")
    f = lax.axis_index("freq")
    core = b % 2
    has_low = b >= 2
    has_high = b + 2 < nchan
    has_up = has_high | (core == 0)
    other = b + 1 - 2 * core
    mine = own_ref.shape[1]
    seg_count, cols = w_ref.shape[1:]
    per = mine // chunks

    barrier = pltpu.get_barrier_semaphore()
    for k in range(1, nfreq):
        pl.semaphore_signal(barrier, inc=1, device_id=(b, peer_of(f, k)), device_id_type=MESH)
    pl.semaphore_signal(barrier, inc=1, device_id=(other, f), device_id_type=MESH)

    @pl.when(has_low)
    def _():
        pl.semaphore_signal(barrier, inc=1, device_id=(b - 2, f), device_id_type=MESH)

    @pl.when(has_high)
    def _():
        pl.semaphore_signal(barrier, inc=1, device_id=(b + 2, f), device_id_type=MESH)

    greeted = nfreq + has_low.astype(jnp.int32) + has_high.astype(jnp.int32)
    pl.semaphore_wait(barrier, greeted)

    def bins_of(device, c):
        return pl.ds(device * mine + c * per, per)

    def rows(c):
        return pl.ds(c * per, per)

    def across(k, c):
        return pltpu.make_async_remote_copy(
            src_ref=w_ref.at[bins_of(peer_of(f, k), c)], dst_ref=own_ref.at[k, rows(c)],
            send_sem=a_send.at[k, c], recv_sem=a_recv.at[k, c],
            device_id=(b, peer_of(f, k)), device_id_type=MESH)

    def down(k, c):
        return pltpu.make_async_remote_copy(
            src_ref=own_ref.at[k, rows(c)], dst_ref=far_ref.at[k, rows(c)],
            send_sem=z_send.at[k, c], recv_sem=z_recv.at[k, c],
            device_id=(b - 2, f), device_id_type=MESH)

    def beside(src_ref, k, c):
        return pltpu.make_async_remote_copy(
            src_ref=src_ref.at[k, rows(c)], dst_ref=up_ref.at[k, rows(c)],
            send_sem=c_send.at[k, c], recv_sem=c_recv.at[k, c],
            device_id=(other, f), device_id_type=MESH)

    down0 = pltpu.make_async_remote_copy(
        src_ref=w_ref.at[pl.ds(f * mine, mine)], dst_ref=far_ref.at[0],
        send_sem=z0_send, recv_sem=z0_recv,
        device_id=(b - 2, f), device_id_type=MESH)

    def beside0(passed):
        return pltpu.make_async_remote_copy(
            src_ref=far_ref.at[0] if passed else w_ref.at[pl.ds(f * mine, mine)], dst_ref=up_ref.at[0],
            send_sem=c0_send, recv_sem=c0_recv,
            device_id=(other, f), device_id_type=MESH)

    @pl.when(has_low)
    def _():
        down0.start()

    @pl.when(core == 1)
    def _():
        beside0(False).start()

    for c in range(chunks):
        for k in range(1, nfreq):
            across(k, c).start()
    local = pltpu.make_async_copy(w_ref.at[pl.ds(f * mine, mine)], own_ref.at[0], l_sem)
    local.start()
    local.wait()

    def own_chunk(c, carry):
        for k in range(1, nfreq):
            across(k, c).wait_recv()

            @pl.when(has_low)
            def _():
                down(k, c).start()

            @pl.when(core == 1)
            def _():
                beside(own_ref, k, c).start()

        def one_bin(j, inner):
            i = c * (per // 2) + j
            product(own_ref, own_ref, i, first_ref, i)
            return inner

        lax.fori_loop(0, per // 2, one_bin, 0)
        return carry

    lax.fori_loop(0, chunks, own_chunk, 0)

    @pl.when(has_high)
    def _():
        down0.wait_recv()

    @pl.when(has_high & (core == 0))
    def _():
        beside0(True).start()

    @pl.when(has_up)
    def _():
        beside0(True).wait_recv()

    def far_chunk(c, carry):
        for k in range(1, nfreq):
            @pl.when(has_high)
            def _():
                down(k, c).wait_recv()

            @pl.when(has_high & (core == 0))
            def _():
                beside(far_ref, k, c).start()

        for k in range(1, nfreq):
            @pl.when(has_up)
            def _():
                beside(far_ref, k, c).wait_recv()

        def one_bin(j, inner):
            i = c * (per // 2) + j

            @pl.when(has_up)
            def _():
                product(own_ref, up_ref, i, second_ref, i)

            @pl.when(has_high)
            def _():
                product(own_ref, far_ref, i, third_ref, i)

            return inner

        @pl.when(c < chunks - 1)
        def _():
            lax.fori_loop(0, per // 2, one_bin, 0)

        return carry

    lax.fori_loop(0, chunks, far_chunk, 0)

    def settle(c, carry):
        for k in range(1, nfreq):
            across(k, c).wait_send()

            @pl.when(has_low)
            def _():
                down(k, c).wait_send()

            @pl.when(has_high | (core == 1))
            def _():
                beside(far_ref, k, c).wait_send()

        return carry

    lax.fori_loop(0, chunks, settle, 0)

    @pl.when(has_low)
    def _():
        down0.wait_send()

    @pl.when(has_high | (core == 1))
    def _():
        beside0(True).wait_send()


def exchange(whitened, nchan, nfreq):
    _, seg_count, cols = whitened.shape
    mine = ROWS // nfreq
    chunks = CHUNKS
    panel = jax.ShapeDtypeStruct((nfreq, mine, seg_count, cols), jnp.bfloat16)
    bins = mine // 2
    ahead = bins - bins // chunks
    results = [jax.ShapeDtypeStruct((n, cols, 2 * cols), jnp.bfloat16) for n in (bins, ahead, ahead)]
    vmem = pl.BlockSpec(memory_space=pltpu.VMEM)
    pair = pltpu.SemaphoreType.DMA((nfreq, chunks))
    return pl.pallas_call(
        functools.partial(exchange_kernel, nchan, nfreq, chunks),
        out_shape=[panel] * 3 + results,
        in_specs=[vmem],
        out_specs=[vmem] * 6,
        scratch_shapes=[pair] * 6 + [pltpu.SemaphoreType.DMA] * 5,
        compiler_params=pltpu.CompilerParams(
            collective_id=0, has_side_effects=True, vmem_limit_bytes=10 * MIB
        ),
        name="exchange",
    )(whitened)


def cross_kernel(keep_ref, own_ref, up_ref, far_ref, first_ref, second_ref, third_ref, out_ref):
    i = pl.program_id(0)
    done = ((own_ref, first_ref), (up_ref, second_ref), (far_ref, third_ref))
    for d, (right_ref, ahead_ref) in enumerate(done):
        count = ahead_ref.shape[0]

        @pl.when((keep_ref[d] != 0) & (i < count))
        def _():
            out_ref[d, 0] = ahead_ref[jnp.minimum(i, count - 1)]

        if count < first_ref.shape[0]:
            @pl.when((keep_ref[d] != 0) & (i >= count))
            def _():
                product(own_ref, right_ref, i, out_ref, d, 0)

        @pl.when(keep_ref[d] == 0)
        def _():
            out_ref[d] = jnp.zeros(out_ref.shape[1:], jnp.bfloat16)


def cross(keep, *parts):
    nfreq, mine, seg_count, cols = parts[0].shape
    bins = mine // 2
    vmem = pl.BlockSpec(memory_space=pltpu.VMEM)
    return pl.pallas_call(
        cross_kernel,
        grid=(bins,),
        out_shape=jax.ShapeDtypeStruct((BAND + 1, bins, cols, 2 * cols), jnp.bfloat16),
        in_specs=[pl.BlockSpec(memory_space=pltpu.SMEM)] + [vmem] * 6,
        out_specs=pl.BlockSpec((BAND + 1, 1, cols, 2 * cols), lambda i: (0, i, 0, 0)),
        compiler_params=pltpu.CompilerParams(vmem_limit_bytes=15 * MIB),
        cost_estimate=pl.CostEstimate(
            flops=3 * bins * cols * cols * 2 * nfreq * seg_count, bytes_accessed=26 * MIB, transcendentals=0
        ),
        name="cross",
    )(keep, *parts)


def shards(nchan, nfreq, records, offsets, dead_mask, band_blocks):
    parts = exchange(whiten(records, offsets, dead_mask), nchan, nfreq)
    b = lax.axis_index("chan")
    offset = jnp.arange(BAND + 1, dtype=jnp.int32)
    keep = ((offset <= band_blocks[0]) & (b + offset < nchan)).astype(jnp.int32)
    return cross(keep, *parts)


def solution(mesh):
    in_specs = (P("freq", "chan"), P("freq"), P("chan"), P("chan"))
    out_specs = P(None, "freq", "chan", None)
    body = functools.partial(shards, mesh.shape["chan"], mesh.shape["freq"])
    return jax.shard_map(body, mesh=mesh, in_specs=in_specs, out_specs=out_specs, check_vma=False)
```

time: 149 us -> 126 us (0.85)
  the two profiles are of different devices: /device:TPU:13 before, /device:TPU:0 now
where the time goes in v2:
time: 126 us; the launch traced here: 125 us
  Pallas kernels  118 us (94%)
  local copies, waits for them, and re-layouts  5.83 us (5%)
    pallas_call x1, Pallas kernels, exchange(): pl.pallas_call(functools.partial(exchange_kernel, nchan, nfreq, chunks),...  97.9 us
    pallas_call x1, Pallas kernels, whiten(): pl.pallas_call(whiten_kernel, out_shape=jax.ShapeDtypeStruct((ROWS, seg_c...  10.8 us
    pallas_call x1, Pallas kernels, cross(): pl.pallas_call(cross_kernel, grid=(bins,), out_shape=jax.ShapeDtypeStruct...  9.38 us
    unnamed x8, local copies, waits for them, and re-layouts  5.83 us

profile of v2, /device:TPU:0, one launch (start us, length us, event | category | flops | bytes accessed | tf_op | source)
XLA Modules:
  0.0 124.6 jit_solution(10268262209998612240)
XLA Ops:
  0.7 0.0 copy-start
  0.7 3.4 %copy-done = bf16[8448,512]{1,0:T(8,128)(2,1)S(1)} copy-done((bf16[8448,512]{1,0:T(8,128)(2,1)S(1)}, bf16[8448,512]{1,0:T(8,128)(2,1)}, u32[]{:S(2)}) %copy-start) | copy-done | bytes 8650776
  4.1 0.0 copy-start.1
  4.1 1.0 copy-done.1
  5.2 0.0 copy-start.2
  5.2 0.7 copy-done.2
  5.8 0.0 copy-start.3
  5.9 0.7 copy-done.3
  6.5 10.8 %whiten.1.w_ref = bf16[64,64,512]{2,1,0:T(8,128)(2,1)S(1)} custom-call(s32[64]{0:T(128)S(1)} %copy-done.3, bf16[8448,512]{1,0:T(8,128)(2,1)S(1)} %copy-done, bf16[16,64,256]{2,1,0:T(8,128)(2,1)S(1)} %copy-done.1, s32[1,512]{1,0:T(1,128)S(1)} %bitcast.3), custom_call_target="tpu_custom_call" | custom-call | flops 1073741824 | bytes 13631488 | tf_op jit(solution)/shard_map/whiten/pallas_call | solution.py:81
  17.3 97.9 %exchange.1 = (bf16[4,16,64,512]{3,2,1,0:T(8,128)(2,1)S(1)}, bf16[4,16,64,512]{3,2,1,0:T(8,128)(2,1)S(1)}, bf16[4,16,64,512]{3,2,1,0:T(8,128)(2,1)S(1)}, bf16[8,...) custom-call(bf16[64,64,512]{2,1,0:T(8,128)(2,1)S(1)} %whiten.1.w_ref), custom_call_target="tpu_custom_call" | custom-call | tf_op jit(solution)/shard_map/exchange/pallas_call | solution.py:305
  115.2 9.4 %cross.1 = bf16[3,8,512,1024]{3,2,1,0:T(8,128)(2,1)} custom-call(s32[3]{0:T(128)S(1)} %and_convert_fusion.keep_ref, bf16[4,16,64,512]{3,2,1,0:T(8,128)(2,1)S(1)} %get-tuple-element.11.own_ref, bf16[4,16,64,512]{3,2,1,0:T(8,128)(2,1)S(1)} %get-tuple-element.12.up_ref, bf16[4,16,64,512]{3,2,1,0:T(8,128)(2,1)S(1)} %get-tuple-element.13.far_ref, ...), custom_call_target="tpu_custom_call" | custom-call | flops 3221225472 | bytes 27262976 | tf_op jit(solution)/shard_map/cross/pallas_call | solution.py:342
  (1 shorter events, 0.0 us)
Async XLA Ops:
  0.7 3.5 %copy-start = (bf16[8448,512]{1,0:T(8,128)(2,1)S(1)}, bf16[8448,512]{1,0:T(8,128)(2,1)}, u32[]{:S(2)}) copy-start(bf16[8448,512]{1,0:T(8,128)(2,1)} %x_ref.1) | copy-start | bytes 25952260
  4.1 1.0 copy-start.1
  5.2 0.7 copy-start.2
  5.8 0.7 copy-start.3

commit v3 on v2

--- a/solution.py
+++ b/solution.py
@@ -16,7 +16,6 @@
 ALIGN = 16
 LANES = 128
 GROUP = 16
-CHUNKS = 4
 BAND = 2
 
 EPS_POWER = 1e-06
@@ -59,7 +58,7 @@
                 flat_ref[j, pl.ds(s, ROWS, stride=GROUP), :] = scaled[:, j * LANES:(j + 1) * LANES]
             return carry
 
-        lax.fori_loop(0, GROUP, segment, 0, unroll=4)
+        lax.fori_loop(0, GROUP, segment, 0, unroll=8)
 
         def pack(r, carry):
             at = pl.ds(pl.multiple_of(r * GROUP, GROUP), GROUP)
@@ -295,7 +294,7 @@
 def exchange(whitened, nchan, nfreq):
     _, seg_count, cols = whitened.shape
     mine = ROWS // nfreq
-    chunks = CHUNKS
+    chunks = mine // 2
     panel = jax.ShapeDtypeStruct((nfreq, mine, seg_count, cols), jnp.bfloat16)
     bins = mine // 2
     ahead = bins - bins // chunks

time: 126 us -> 125 us (level)
  no operation moved by 1% of the time
where the time goes in v3:
time: 125 us; the launch traced here: 124 us
  Pallas kernels  118 us (94%)
  local copies, waits for them, and re-layouts  5.83 us (5%)
    pallas_call x1, Pallas kernels, exchange(): pl.pallas_call(functools.partial(exchange_kernel, nchan, nfreq, chunks),...  98.6 us
    pallas_call x1, Pallas kernels, whiten(): pl.pallas_call(whiten_kernel, out_shape=jax.ShapeDtypeStruct((ROWS, seg_c...  9.59 us
    pallas_call x1, Pallas kernels, cross(): pl.pallas_call(cross_kernel, grid=(bins,), out_shape=jax.ShapeDtypeStruct...  9.38 us
    unnamed x8, local copies, waits for them, and re-layouts  5.83 us

profile of v3, /device:TPU:0, one launch (start us, length us, event | category | flops | bytes accessed | tf_op | source)
XLA Modules:
  0.0 124.1 jit_solution(17504011849310440724)
XLA Ops:
  0.7 0.0 copy-start
  0.7 3.4 %copy-done = bf16[8448,512]{1,0:T(8,128)(2,1)S(1)} copy-done((bf16[8448,512]{1,0:T(8,128)(2,1)S(1)}, bf16[8448,512]{1,0:T(8,128)(2,1)}, u32[]{:S(2)}) %copy-start) | copy-done | bytes 8650776
  4.1 0.0 copy-start.1
  4.1 1.0 copy-done.1
  5.2 0.0 copy-start.2
  5.2 0.7 copy-done.2
  5.8 0.0 copy-start.3
  5.9 0.7 copy-done.3
  6.5 9.6 %whiten.1.w_ref = bf16[64,64,512]{2,1,0:T(8,128)(2,1)S(1)} custom-call(s32[64]{0:T(128)S(1)} %copy-done.3, bf16[8448,512]{1,0:T(8,128)(2,1)S(1)} %copy-done, bf16[16,64,256]{2,1,0:T(8,128)(2,1)S(1)} %copy-done.1, s32[1,512]{1,0:T(1,128)S(1)} %bitcast.3), custom_call_target="tpu_custom_call" | custom-call | flops 1073741824 | bytes 13631488 | tf_op jit(solution)/shard_map/whiten/pallas_call | solution.py:80
  16.1 98.6 %exchange.1 = (bf16[4,16,64,512]{3,2,1,0:T(8,128)(2,1)S(1)}, bf16[4,16,64,512]{3,2,1,0:T(8,128)(2,1)S(1)}, bf16[4,16,64,512]{3,2,1,0:T(8,128)(2,1)S(1)}, bf16[8,...) custom-call(bf16[64,64,512]{2,1,0:T(8,128)(2,1)S(1)} %whiten.1.w_ref), custom_call_target="tpu_custom_call" | custom-call | tf_op jit(solution)/shard_map/exchange/pallas_call | solution.py:304
  114.7 9.4 %cross.1 = bf16[3,8,512,1024]{3,2,1,0:T(8,128)(2,1)} custom-call(s32[3]{0:T(128)S(1)} %and_convert_fusion.keep_ref, bf16[4,16,64,512]{3,2,1,0:T(8,128)(2,1)S(1)} %get-tuple-element.11.own_ref, bf16[4,16,64,512]{3,2,1,0:T(8,128)(2,1)S(1)} %get-tuple-element.12.up_ref, bf16[4,16,64,512]{3,2,1,0:T(8,128)(2,1)S(1)} %get-tuple-element.13.far_ref, ...), custom_call_target="tpu_custom_call" | custom-call | flops 3221225472 | bytes 27262976 | tf_op jit(solution)/shard_map/cross/pallas_call | solution.py:341
  (1 shorter events, 0.0 us)
Async XLA Ops:
  0.7 3.5 %copy-start = (bf16[8448,512]{1,0:T(8,128)(2,1)S(1)}, bf16[8448,512]{1,0:T(8,128)(2,1)}, u32[]{:S(2)}) copy-start(bf16[8448,512]{1,0:T(8,128)(2,1)} %x_ref.1) | copy-start | bytes 25952260
  4.1 1.0 copy-start.1
  5.2 0.7 copy-start.2
  5.8 0.7 copy-start.3
